TPU v7x, 32 devices: a whole 2x2x4 slice. The times are simulated.
32 devices in a mesh: groups: 2 (over y), rows: 4 (over z), cols: 4 (over x, core).
Axes of the slice: x: 2, y: 2, z: 4, core: 2. Of those that a mesh axis runs over, the one named last changes fastest.
Arguments:
- hidden: bfloat16 [64, 32, 1280], P(('groups', 'rows'), 'cols'), parts along dimension 0, may hold values from -6 to 6
- ln_gain: float32 [1280], replicated, may hold values from 0.1 to 1.9
- ln_bias: float32 [1280], replicated, may hold values from -3 to 3
- w_query: bfloat16 [1280, 256], P(None, 'cols'), may hold values from -8.944272 to 8.944272
- w_keyval: bfloat16 [1280, 512], P(None, 'cols'), may hold values from -0.3125 to 0.3125
- stale_keyval: bfloat16 [64, 32, 4, 128], P(('groups', 'rows'), None, 'cols'), parts along dimension 0, may hold values from -10 to 10
- w_out: bfloat16 [256, 1280], replicated, may hold values from -0.375 to 0.375
- out_bias: float32 [1280], replicated, may hold values from -3 to 3
Outputs:
- output_rows: bfloat16 [64, 32, 1280], P(('groups', 'rows'), 'cols'), parts along dimension 0
- fresh_keyval: bfloat16 [64, 32, 4, 128], P(('groups', 'rows'), None, 'cols'), parts along dimension 0
There are 2 independent parts, one for each index of `groups`. A program takes and returns all parts, laid end to end along the dimension named above; an argument that names none is the same for every part. Nothing has to cross between parts.
All inputs are finite; a program needn't handle non-finite values.
Results may differ from a plain program's by a relative error of at most 0.04.
The roundings to bfloat16 on the way count: a program that leaves them out, or rounds other values in their place, can miss the bound.
Values may be sent and summed in bfloat16 or wider, within the bound.
A program may use at most 64 MiB of HBM per device.

v0:
```python
import math

import jax
import jax.numpy as jnp
from jax import lax
from jax.sharding import PartitionSpec as P


def layer_norm(hidden, ln_gain, ln_bias):
    values = hidden.astype(jnp.float32)
    row_mean = jnp.mean(values, axis=-1, keepdims=True)
    centred = values - row_mean
    variance = jnp.mean(centred * centred, axis=-1, keepdims=True)
    return (centred * lax.rsqrt(variance + 1e-05) * ln_gain + ln_bias).astype(jnp.bfloat16)


def absorb(running, key_block, queries, score_scale):
    row_max, denominator, weighted = running
    head_size = queries.shape[1]
    scores = (
        jnp.dot(queries, key_block[:, :head_size].T, preferred_element_type=jnp.float32)
        * score_scale
    )
    new_max = jnp.maximum(row_max, jnp.max(scores, axis=-1))
    factor = jnp.exp(row_max - new_max)
    probability = jnp.exp(scores - new_max[:, None])
    denominator = denominator * factor + jnp.sum(probability, axis=-1)
    weighted = weighted * factor[:, None] + jnp.dot(
        probability.astype(jnp.bfloat16),
        key_block[:, head_size:],
        preferred_element_type=jnp.float32,
    )
    return (new_max, denominator, weighted)


def shards(hidden, ln_gain, ln_bias, w_query, w_keyval, stale_keyval, w_out, out_bias):
    band_rows, strip_cols, channels = hidden.shape
    head_size = w_query.shape[1]
    normed = layer_norm(hidden, ln_gain, ln_bias)
    both_weights = jnp.concatenate([w_query, w_keyval], axis=1)
    projected = jnp.dot(
        lax.all_gather(normed, "cols", axis=1, tiled=True),
        both_weights,
        preferred_element_type=jnp.float32,
    ).astype(jnp.bfloat16)
    full_cols = projected.shape[1]
    queries = projected[:, :, :head_size].reshape(-1, head_size)
    keyval = projected[:, :, head_size:]
    fresh_flat = keyval.reshape(-1, 2 * head_size)
    own_band = lax.axis_index("rows")
    score_scale = 1.0 / math.sqrt(head_size)
    query_count = queries.shape[0]
    initial = (
        jnp.full((query_count,), -1e30, jnp.float32),
        jnp.zeros((query_count,), jnp.float32),
        jnp.zeros((query_count, head_size), jnp.float32),
    )
    received = lax.all_gather(stale_keyval, "rows", axis=0, tiled=True)
    band_count = received.shape[0] // band_rows
    key_blocks = received.reshape(band_count, band_rows * full_cols, 2 * head_size)

    def step_band(state, position):
        key_block = jnp.where(position == own_band, fresh_flat, key_blocks[position])
        return (absorb(state, key_block, queries, score_scale), None)

    folded, unused = lax.scan(step_band, initial, jnp.arange(band_count, dtype=jnp.int32))
    row_max, denominator, weighted = folded
    attention = (
        (weighted / denominator[:, None])
        .astype(jnp.bfloat16)
        .reshape(band_rows, full_cols, 1, head_size)
    )
    values = lax.all_to_all(attention, "cols", split_axis=1, concat_axis=2, tiled=True)
    row_count = values.shape[0]
    flat_values = values.reshape(row_count * values.shape[1], values.shape[2] * values.shape[3])
    result = jnp.dot(flat_values, w_out, preferred_element_type=jnp.float32)
    projected_out = result.reshape(row_count, values.shape[1], channels)
    output_rows = (projected_out + out_bias + hidden.astype(jnp.float32)).astype(jnp.bfloat16)
    return (output_rows, keyval.reshape(band_rows, full_cols, 1, 2 * head_size))


def solution(mesh):
    return jax.shard_map(
        shards,
        mesh=mesh,
        in_specs=(
            P(("groups", "rows"), "cols", None),
            P(),
            P(),
            P(None, "cols"),
            P(None, "cols"),
            P(("groups", "rows"), None, "cols", None),
            P(),
            P(),
        ),
        out_specs=(P(("groups", "rows"), "cols", None), P(("groups", "rows"), None, "cols", None)),
        check_vma=False,
    )
```

profile of v0, /device:TPU:0, one launch (start us, length us, event | category | flops | bytes accessed | tf_op | source)
XLA Modules:
  0.0 53.2 jit_solution(13207126210081687228)
XLA Ops:
  0.7 1.1 %convert_reduce_fusion = f32[8,8]{1,0:T(8,128)S(1)} fusion(bf16[8,8,1280]{2,1,0:T(8,128)(2,1)} %param.10), kind=kLoop, calls=%fused_computation.24 | loop fusion | flops 163776 | bytes 164096 | tf_op jit(solution)/shard_map/reduce_sum | solution.py:11
  1.8 0.2 fusion.15
  2.0 0.5 copy-done.7
  2.5 0.2 copy-done.6
  2.7 0.1 fusion.18
  2.8 9.5 %all_gather.7 = bf16[8,32,1280]{2,1,0:T(8,128)(2,1)S(1)} all-gather(bf16[8,8,1280]{2,1,0:T(8,128)(2,1)S(1)} %fusion.18), channel_id=1, replica_groups=mesh['groups'=2,'rows'=4,'cols'=4] {'cols'}, dimensions={1}, use_global_device_ids=true | all-gather | bytes 819200 | tf_op jit(solution)/shard_map/all_gather | solution.py:42
  12.3 0.2 copy.16
  12.5 0.7 %copy-done.8 = bf16[1280,64]{0,1:T(8,128)(2,1)S(1)} copy-done((bf16[1280,64]{0,1:T(8,128)(2,1)S(1)}, bf16[1280,64]{0,1:T(8,128)(2,1)}, u32[]{:S(2)}) %copy-start.8) | copy-done | bytes 163864
  13.2 0.3 convolution_convert_fusion
  13.6 0.7 %slice_bitcast_fusion = (bf16[8,32,1,128]{3,1,2,0:T(8,128)(2,1)}, bf16[8,32,128]{2,1,0:T(8,128)(2,1)S(1)}) fusion(bf16[8,32,192]{2,1,0:T(8,128)(2,1)S(1)} %convolution_convert_fusion), kind=kLoop, calls=%fused_computation.36 | loop fusion | bytes 196608
  14.3 0.8 %copy-done.4 = bf16[8,32,1,128]{3,1,2,0:T(8,128)(2,1)S(1)} copy-done((bf16[8,32,1,128]{3,1,2,0:T(8,128)(2,1)S(1)}, bf16[8,32,1,128]{3,1,2,0:T(8,128)(2,1)}, u32[]{:S(2)}) %copy-start.4) | copy-done | bytes 65560
  15.1 14.2 %all_gather.6 = bf16[32,32,1,128]{3,1,2,0:T(8,128)(2,1)S(1)} all-gather(bf16[8,32,1,128]{3,1,2,0:T(8,128)(2,1)S(1)} %copy-done.4), channel_id=1, replica_groups=mesh['groups'=2,'rows'=4,'cols'=4] {'rows'}, dimensions={0}, use_global_device_ids=true | all-gather | bytes 327680 | tf_op jit(solution)/shard_map/all_gather | solution.py:58
  29.4 15.4 %while.15 = (s32[]{:T(128)}, f32[256]{0:T(256)S(1)}, f32[256]{0:T(256)S(1)}, f32[256,64]{0,1:T(8,128)S(1)}, s32[4]{0:T(128)S(1)}, /*index=5*/s32[]{:T(128)}, bf1...) while((s32[]{:T(128)}, f32[256]{0:T(256)S(1)}, ...), condition=%wide.region_5.6_spmd.clone, body=%wide.region_2.5_spmd.clone.sunk | while | flops 17253640 | bytes 1294525 | solution.py:66
  29.4 0.6 %dynamic_slice.13 = s32[1]{0:T(128)} dynamic-slice(s32[4]{0:T(128)S(1)} %get-tuple-element.203, s32[]{:T(128)} %get-tuple-element.187), dynamic_slice_sizes={1} | dynamic-slice | bytes 12 | tf_op jit(solution)/shard_map/while/body/jit(dynamic_index_in_dim)/dynamic_slice | solution.py:66
  32.6 0.2 fusion.34
  32.9 0.3 convolution_add_fusion.3
  33.2 0.6 %dynamic_slice.13 = s32[1]{0:T(128)} dynamic-slice(s32[4]{0:T(128)S(1)} %get-tuple-element.203, s32[]{:T(128)} %get-tuple-element.187), dynamic_slice_sizes={1} | dynamic-slice | bytes 12 | tf_op jit(solution)/shard_map/while/body/jit(dynamic_index_in_dim)/dynamic_slice | solution.py:66
  36.4 0.2 fusion.34
  36.8 0.3 convolution_add_fusion.3
  37.1 0.6 %dynamic_slice.13 = s32[1]{0:T(128)} dynamic-slice(s32[4]{0:T(128)S(1)} %get-tuple-element.203, s32[]{:T(128)} %get-tuple-element.187), dynamic_slice_sizes={1} | dynamic-slice | bytes 12 | tf_op jit(solution)/shard_map/while/body/jit(dynamic_index_in_dim)/dynamic_slice | solution.py:66
  40.3 0.2 fusion.34
  40.6 0.3 convolution_add_fusion.3
  40.9 0.6 %dynamic_slice.13 = s32[1]{0:T(128)} dynamic-slice(s32[4]{0:T(128)S(1)} %get-tuple-element.203, s32[]{:T(128)} %get-tuple-element.187), dynamic_slice_sizes={1} | dynamic-slice | bytes 12 | tf_op jit(solution)/shard_map/while/body/jit(dynamic_index_in_dim)/dynamic_slice | solution.py:66
  44.1 0.2 fusion.34
  44.5 0.3 convolution_add_fusion.3
  44.9 0.1 divide_convert_fusion
  45.0 0.1 reshape.49
  45.1 6.3 %all_to_all.15 = bf16[4,2,2048]{2,1,0:T(2,128)(2,1)S(1)} all-to-all(bf16[4,2,2048]{2,1,0:T(2,128)(2,1)S(1)} %reshape.49), channel_id=1, replica_groups=mesh['groups'=2,'rows'=4,'cols'=4] {'cols'}, dimensions={0} | all-to-all | bytes 65536 | tf_op jit(solution)/shard_map/all_to_all | solution.py:73
  51.4 0.1 reshape.50
  51.6 0.1 dot_general.15
  51.7 0.6 %copy-done.5 = f32[1280]{0:T(1024)S(1)} copy-done((f32[1280]{0:T(1024)S(1)}, f32[1280]{0:T(1024)}, u32[]{:S(2)}) %copy-start.5) | copy-done | bytes 5144
  52.3 0.9 %fusion.9 = bf16[8,8,1280]{2,1,0:T(8,128)(2,1)} fusion(bf16[8,8,256]{2,1,0:T(8,128)(2,1)S(1)} %dot_general.15, bf16[256,1280]{1,0:T(8,128)(2,1)S(1)} %copy-done, bf16[8,8,1280]{2,1,0:T(8,128)(2,1)S(1)} %copy-done.1, f32[1280]{0:T(1024)S(1)} %copy-done.5), kind=kOutput, calls=%fused_computation.17 | convolution fusion | flops 42270720 | bytes 1020928 | tf_op jit(solution)/shard_map/dot_general | solution.py:76
  (45 shorter events, 0.7 us)
Async XLA Ops:
  0.6 51.1 %copy-start = (bf16[256,1280]{1,0:T(8,128)(2,1)S(1)}, bf16[256,1280]{1,0:T(8,128)(2,1)}, u32[]{:S(2)}) copy-start(bf16[256,1280]{1,0:T(8,128)(2,1)} %param.16) | copy-start | bytes 1966084
  0.6 1.1 %copy-start.1 = (bf16[8,8,1280]{2,1,0:T(8,128)(2,1)S(1)}, bf16[8,8,1280]{2,1,0:T(8,128)(2,1)}, u32[]{:S(2)}) copy-start(bf16[8,8,1280]{2,1,0:T(8,128)(2,1)} %param.10) | copy-start | bytes 491524
  1.8 0.7 %copy-start.7 = (f32[1280]{0:T(1024)S(1)}, f32[1280]{0:T(1024)}, u32[]{:S(2)}) copy-start(f32[1280]{0:T(1024)} %param.11) | copy-start | bytes 15364
  2.0 0.7 %copy-start.6 = (f32[1280]{0:T(1024)S(1)}, f32[1280]{0:T(1024)}, u32[]{:S(2)}) copy-start(f32[1280]{0:T(1024)} %param.12) | copy-start | bytes 15364
  2.8 9.5 %copy-start.3 = (bf16[1280,128]{1,0:T(8,128)(2,1)S(1)}, bf16[1280,128]{1,0:T(8,128)(2,1)}, u32[]{:S(2)}) copy-start(bf16[1280,128]{1,0:T(8,128)(2,1)} %param.14) | copy-start | bytes 983044
  12.3 0.9 %copy-start.8 = (bf16[1280,64]{0,1:T(8,128)(2,1)S(1)}, bf16[1280,64]{0,1:T(8,128)(2,1)}, u32[]{:S(2)}) copy-start(bf16[1280,64]{0,1:T(8,128)(2,1)} %param.13) | copy-start | bytes 491524
  13.5 0.7 %copy-start.2 = (bf16[8,32,192]{2,1,0:T(8,128)(2,1)}, bf16[8,32,192]{2,1,0:T(8,128)(2,1)S(1)}, u32[]{:S(2)}) copy-start(bf16[8,32,192]{2,1,0:T(8,128)(2,1)S(1)} %convolution_convert_fusion) | copy-start | bytes 294916
  14.3 0.8 %copy-start.4 = (bf16[8,32,1,128]{3,1,2,0:T(8,128)(2,1)S(1)}, bf16[8,32,1,128]{3,1,2,0:T(8,128)(2,1)}, u32[]{:S(2)}) copy-start(bf16[8,32,1,128]{3,1,2,0:T(8,128)(2,1)} %param.15) | copy-start | bytes 196612
  15.1 14.2 %slice-start = ((bf16[8,32,192]{2,1,0:T(8,128)(2,1)}), bf16[8,32,64]{2,1,0:T(8,128)(2,1)S(1)}, s32[]{:S(2)}) async-start(bf16[8,32,192]{2,1,0:T(8,128)(2,1)} %copy-done.2), calls=%async_computation.1 | async-start | bytes 131072 | tf_op jit(solution)/shard_map/slice | solution.py:47
  51.6 0.7 %copy-start.5 = (f32[1280]{0:T(1024)S(1)}, f32[1280]{0:T(1024)}, u32[]{:S(2)}) copy-start(f32[1280]{0:T(1024)} %param.17) | copy-start | bytes 15364
where the time goes:
time: 53.8 us; the launch traced here: 53.2 us
  blocking collectives  30 us (56%)
  loops' own time  10.6 us (20%)
  local copies, waits for them, and re-layouts  6.62 us (12%)
  matrix products  3.29 us (6%)
  other arithmetic  1.97 us (4%)
  between operations  0.77 us (1%)
    all_gather x1, blocking collectives, shards(): received = lax.all_gather(stale_keyval, 'rows', axis=0, tiled=True)  14.2 us
    another operation x1, loops' own time, shards(): lax.scan(step_band, initial, jnp.arange(band_count, dtype=jnp.int32))  10.6 us
    all_gather x1, blocking collectives, shards(): lax.all_gather(normed, 'cols', axis=1, tiled=True)  9.46 us
    all_to_all x1, blocking collectives, shards(): lax.all_to_all(attention, 'cols', split_axis=1, concat_axis=2, tiled=True)  6.3 us
    unnamed x22, local copies, waits for them, and re-layouts  3.99 us
    dynamic_slice x4, local copies, waits for them, and re-layouts, shards(): lax.scan(step_band, initial, jnp.arange(band_count, dtype=jnp.int32))  2.34 us
    dot_general x4, matrix products, absorb(): jnp.dot(probability.astype(jnp.bfloat16), key_block[:, head_size:], prefe...  1.16 us
    reduce_sum x1, other arithmetic, layer_norm(): row_mean = jnp.mean(values, axis=-1, keepdims=True)  1.1 us

commit v1 on v0

v1 whole, which is shorter than its diff:
```python
import functools
import math

import jax
import jax.numpy as jnp
from jax import lax
from jax.experimental import pallas as pl
from jax.experimental.pallas import tpu as pltpu
from jax.sharding import PartitionSpec as P

MESH = pl.DeviceIdType.MESH
PIECES = 4


def repeat(count, body):
    if count <= 4:
        for index in range(count):
            body(index)
    else:
        lax.fori_loop(0, count, lambda index, carry: (body(index), carry)[1], 0)


def kernel(
    n_rows, n_cols, cores,
    hidden_hbm, gain_ref, bias_ref, w_query_hbm, w_keyval_hbm, stale_hbm, w_out_hbm, out_bias_ref,
    out_hbm, fresh_hbm,
    hidden, w_query, w_keyval, w_out, normed, queries, keyval, fresh_wide, fresh, out, attention,
    load_sem, band_send, band_recv, strip_send, strip_recv, relay_send, relay_recv, att_send, att_recv, store_sem,
):
    row = lax.axis_index("rows")
    col = lax.axis_index("cols")
    chips = n_cols // cores
    chip, core = col // cores, col % cores
    sibling = chip * cores + (cores - 1 - core)
    band_rows, strip_cols, channels = hidden.shape
    strip = band_rows * strip_cols
    pair = cores * strip
    head_size = w_query.shape[1]
    piece = strip // PIECES
    scale = 1.0 / math.sqrt(head_size)

    loads = [
        pltpu.make_async_copy(source, target, load_sem.at[index])
        for index, (source, target) in enumerate(
            [
                (hidden_hbm, hidden),
                (w_query_hbm, w_query),
                (w_keyval_hbm, w_keyval),
                (w_out_hbm, w_out),
            ]
        )
    ]
    for load in loads:
        load.start()

    barrier = pltpu.get_barrier_semaphore()

    def greet_col(step):
        pl.semaphore_signal(
            barrier, inc=1, device_id={"cols": lax.rem(col + step + 1, n_cols)}, device_id_type=MESH
        )

    def greet_row(step):
        pl.semaphore_signal(
            barrier, inc=1, device_id={"rows": lax.rem(row + step + 1, n_rows)}, device_id_type=MESH
        )

    repeat(n_cols - 1, greet_col)
    repeat(n_rows - 1, greet_row)

    loads[0].wait()
    values = hidden[...].astype(jnp.float32).reshape(strip, channels)
    centred = values - jnp.mean(values, axis=-1, keepdims=True)
    variance = jnp.mean(centred * centred, axis=-1, keepdims=True)
    own_rows = pl.ds(pl.multiple_of(core * strip, strip), strip)
    normed[chip, own_rows, :] = (
        centred * lax.rsqrt(variance + 1e-05) * gain_ref[...] + bias_ref[...]
    ).astype(jnp.bfloat16)
    pl.semaphore_wait(barrier, n_cols - 1 + n_rows - 1)

    def rows_of(core_index, part):
        return pl.ds(pl.multiple_of(core_index * strip + part * piece, piece), piece)

    def strip_copy(step, part):
        other = lax.rem(chip + step + 1, chips)
        block = normed.at[chip, rows_of(core, part), :]
        return pltpu.make_async_remote_copy(
            src_ref=block, dst_ref=block,
            send_sem=strip_send.at[step, part], recv_sem=strip_recv.at[step, part],
            device_id={"cols": other * cores + core}, device_id_type=MESH,
        )

    def relay_copy(step, part):
        source_chip = lax.rem(chip + chips - step, chips)
        block = normed.at[source_chip, rows_of(core, part), :]
        return pltpu.make_async_remote_copy(
            src_ref=block, dst_ref=block,
            send_sem=relay_send.at[step, part], recv_sem=relay_recv.at[step, part],
            device_id={"cols": sibling}, device_id_type=MESH,
        )

    def band_copy(step):
        return pltpu.make_async_remote_copy(
            src_ref=stale_hbm, dst_ref=keyval.at[row],
            send_sem=band_send.at[step], recv_sem=band_recv.at[step],
            device_id={"rows": lax.rem(row + step + 1, n_rows)}, device_id_type=MESH,
        )

    for part in range(PIECES):
        repeat(chips - 1, lambda step, part=part: strip_copy(step, part).start())
    if cores > 1:
        for part in range(PIECES):
            relay_copy(0, part).start()
    repeat(n_rows - 1, lambda step: band_copy(step).start())

    def project(index):
        rows = normed[index]
        own = jnp.dot(rows, w_query[...], preferred_element_type=jnp.float32).astype(jnp.bfloat16)
        queries[index] = jnp.concatenate([own, jnp.zeros_like(own)], axis=1)
        both = jnp.dot(rows, w_keyval[...], preferred_element_type=jnp.float32).astype(jnp.bfloat16)
        keyval[row, pl.ds(pl.multiple_of(index * pair, pair), pair), :] = both
        wide = both.astype(jnp.float32).reshape(cores, band_rows, strip_cols, both.shape[1])
        for which in range(cores):
            fresh_wide[:, index * cores + which] = wide[which]

    for load in loads[1:3]:
        load.wait()
    if cores > 1:
        for part in range(PIECES):
            relay_copy(0, part).wait_recv()
    project(chip)

    def arrive(step):
        for part in range(PIECES):
            strip_copy(step, part).wait_recv()
            if cores > 1:
                relay_copy(step + 1, part).start()
        if cores > 1:
            for part in range(PIECES):
                relay_copy(step + 1, part).wait_recv()
        project(lax.rem(chip + chips - step - 1, chips))

    repeat(chips - 1, arrive)

    fresh[...] = fresh_wide[...].reshape(fresh.shape).astype(jnp.bfloat16)
    fresh_store = pltpu.make_async_copy(fresh, fresh_hbm, store_sem.at[0])
    fresh_store.start()

    repeat(n_rows - 1, lambda step: band_copy(step).wait_recv())

    cells = keyval.shape[1]
    together = max(size for size in range(1, n_rows + 1) if n_rows % size == 0 and (size == 1 or size * cells <= 1024))

    def absorb(own, index):
        block = keyval[pl.ds(index * together, together)].reshape(together * cells, keyval.shape[2])
        scores = lax.dot_general(
            own, block, (((1,), (1,)), ((), ())), preferred_element_type=jnp.float32
        )
        return block, scores

    def attend(index):
        own = queries[index]
        if together == n_rows:
            block, scores = absorb(own, 0)
            row_max = jnp.max(scores, axis=-1, keepdims=True)
            weights = jnp.exp((scores - row_max) * scale)
            denominator = jnp.sum(weights, axis=-1, keepdims=True)
            weighted = jnp.dot(weights.astype(jnp.bfloat16), block, preferred_element_type=jnp.float32)
        else:

            def body(step, state):
                row_max, denominator, weighted = state
                block, scores = absorb(own, step)
                new_max = jnp.maximum(row_max, jnp.max(scores, axis=-1, keepdims=True))
                factor = jnp.exp((row_max - new_max) * scale)
                weights = jnp.exp((scores - new_max) * scale)
                return (
                    new_max,
                    denominator * factor + jnp.sum(weights, axis=-1, keepdims=True),
                    weighted * factor
                    + jnp.dot(weights.astype(jnp.bfloat16), block, preferred_element_type=jnp.float32),
                )

            initial = (
                jnp.full((pair, 1), -1e30, jnp.float32),
                jnp.zeros((pair, 1), jnp.float32),
                jnp.zeros((pair, 2 * head_size), jnp.float32),
            )
            row_max, denominator, weighted = lax.fori_loop(0, n_rows // together, body, initial)
        return (weighted[:, head_size:] / denominator).astype(jnp.bfloat16)

    def att_copy(target, step):
        return pltpu.make_async_remote_copy(
            src_ref=attention.at[0, target], dst_ref=attention.at[1, col],
            send_sem=att_send.at[step], recv_sem=att_recv.at[step],
            device_id={"cols": target}, device_id_type=MESH,
        )

    def serve(step):
        other = lax.rem(chip + step + 1, chips)
        found = attend(other)
        for which in range(cores):
            target = other * cores + lax.rem(core + which, cores)
            attention[0, other * cores + which] = found[which * strip : (which + 1) * strip]
        for which in range(cores):
            target = other * cores + lax.rem(core + which, cores)
            att_copy(target, (step + 1) * cores + which).start()

    repeat(chips - 1, serve)
    found = attend(chip)
    for which in range(cores):
        attention[0, chip * cores + which] = found[which * strip : (which + 1) * strip]
    if cores > 1:
        att_copy(sibling, 1).start()
    attention[1, col] = attention[0, col]

    loads[3].wait()
    if cores > 1:
        att_copy(sibling, 1).wait_recv()
    for step in range(cores, n_cols):
        att_copy(sibling, step).wait_recv()
    together_heads = jnp.concatenate([attention[1, head] for head in range(n_cols)], axis=1)
    result = jnp.dot(together_heads, w_out[...], preferred_element_type=jnp.float32)
    result = result + out_bias_ref[...] + hidden[...].astype(jnp.float32).reshape(strip, channels)
    out[...] = result.reshape(out.shape).astype(jnp.bfloat16)
    out_store = pltpu.make_async_copy(out, out_hbm, store_sem.at[1])
    out_store.start()

    for part in range(PIECES):
        repeat(chips - 1, lambda step, part=part: strip_copy(step, part).wait_send())
        if cores > 1:
            repeat(chips, lambda step, part=part: relay_copy(step, part).wait_send())
    repeat(n_rows - 1, lambda step: band_copy(step).wait_send())
    for step in range(1, n_cols):
        att_copy(sibling, step).wait_send()
    fresh_store.wait()
    out_store.wait()


def shards(n_rows, n_cols, hidden, ln_gain, ln_bias, w_query, w_keyval, stale_keyval, w_out, out_bias):
    band_rows, strip_cols, channels = hidden.shape
    head_size = w_query.shape[1]
    full_cols = stale_keyval.shape[1]
    cells = band_rows * full_cols
    strip = band_rows * strip_cols
    cores = 2 if n_cols % 2 == 0 else 1
    chips = n_cols // cores
    bf16, f32 = jnp.bfloat16, jnp.float32
    anywhere = pl.BlockSpec(memory_space=pl.ANY)
    near = pl.BlockSpec(memory_space=pltpu.VMEM)
    dma = pltpu.SemaphoreType.DMA
    out, fresh = pl.pallas_call(
        functools.partial(kernel, n_rows, n_cols, cores),
        out_shape=(
            jax.ShapeDtypeStruct(hidden.shape, bf16),
            jax.ShapeDtypeStruct((band_rows, full_cols, 2 * head_size), bf16),
        ),
        in_specs=[anywhere, near, near, anywhere, anywhere, anywhere, anywhere, near],
        out_specs=(anywhere, anywhere),
        scratch_shapes=[
            pltpu.VMEM(hidden.shape, bf16),
            pltpu.VMEM(w_query.shape, bf16),
            pltpu.VMEM(w_keyval.shape, bf16),
            pltpu.VMEM(w_out.shape, bf16),
            pltpu.VMEM((chips, cores * strip, channels), bf16),
            pltpu.VMEM((chips, cores * strip, 2 * head_size), bf16),
            pltpu.VMEM((n_rows, cells, 2 * head_size), bf16),
            pltpu.VMEM((band_rows, n_cols, strip_cols, 2 * head_size), f32),
            pltpu.VMEM((band_rows, full_cols, 2 * head_size), bf16),
            pltpu.VMEM(hidden.shape, bf16),
            pltpu.VMEM((2, n_cols, strip, head_size), bf16),
            dma((4,)),
            dma((n_rows,)),
            dma((n_rows,)),
            dma((chips, PIECES)),
            dma((chips, PIECES)),
            dma((chips, PIECES)),
            dma((chips, PIECES)),
            dma((n_cols,)),
            dma((n_cols,)),
            dma((2,)),
        ],
        compiler_params=pltpu.CompilerParams(
            collective_id=0, has_side_effects=True, vmem_limit_bytes=48 * 1024 * 1024
        ),
    )(
        hidden,
        ln_gain.reshape(1, channels),
        ln_bias.reshape(1, channels),
        w_query,
        w_keyval,
        stale_keyval.reshape(cells, 2 * head_size),
        w_out,
        out_bias.reshape(1, channels),
    )
    return out, fresh.reshape(band_rows, full_cols, 1, 2 * head_size)


def solution(mesh):
    return jax.shard_map(
        functools.partial(shards, mesh.shape["rows"], mesh.shape["cols"]),
        mesh=mesh,
        in_specs=(
            P(("groups", "rows"), "cols", None),
            P(),
            P(),
            P(None, "cols"),
            P(None, "cols"),
            P(("groups", "rows"), None, "cols", None),
            P(),
            P(),
        ),
        out_specs=(P(("groups", "rows"), "cols", None), P(("groups", "rows"), None, "cols", None)),
        check_vma=False,
    )
```

time: 53.8 us -> 24 us (0.45)
  blocking collectives: 30 us -> 0 us
  Pallas kernels: 0 us -> 16.4 us
  loops' own time: 10.6 us -> 0 us
  matrix products: 3.29 us -> 0 us
  other arithmetic: 1.97 us -> 0 us
    all_gather x2 -> x0, blocking collectives: 23.7 us -> none  [the longest x1 14.2 us: shards(): received = lax.all_gather(stale_keyval, 'rows', axis=0, tiled=True)]
    pallas_call x0 -> x1, Pallas kernels: none -> 16.4 us  [shards(): pl.pallas_call(functools.partial(kernel, n_rows, n_cols, cores), out_shap...]
    another operation x1 -> x0, loops' own time: 10.6 us -> none  [shards(): lax.scan(step_band, initial, jnp.arange(band_count, dtype=jnp.int32))]
    all_to_all x1 -> x0, blocking collectives: 6.3 us -> none  [shards(): lax.all_to_all(attention, 'cols', split_axis=1, concat_axis=2, tiled=True)]
    dot_general x10 -> x0, matrix products: 3.29 us -> none  [the longest x4 1.16 us: absorb(): jnp.dot(probability.astype(jnp.bfloat16), key_block[:, head_size:], prefe...]
    dynamic_slice x4 -> x0, local copies, waits for them, and re-layouts: 2.34 us -> none  [shards(): lax.scan(step_band, initial, jnp.arange(band_count, dtype=jnp.int32))]
    reshape x1 -> x3, local copies, waits for them, and re-layouts: 0.03 us -> 2.15 us  [the longest x1 0.75 us: shards(): ln_gain.reshape(1, channels)]
    reduce_sum x6 -> x0, other arithmetic: 1.58 us -> none  [the longest x1 1.1 us: layer_norm(): row_mean = jnp.mean(values, axis=-1, keepdims=True)]
where the time goes in v1:
time: 24 us; the launch traced here: 23.6 us
  Pallas kernels  16.4 us (68%)
  local copies, waits for them, and re-layouts  6.55 us (27%)
  between operations  0.68 us (3%)
    pallas_call x1, Pallas kernels, shards(): pl.pallas_call(functools.partial(kernel, n_rows, n_cols, cores), out_shap...  16.4 us
    unnamed x11, local copies, waits for them, and re-layouts  4.4 us
    reshape x1, local copies, waits for them, and re-layouts, shards(): ln_gain.reshape(1, channels)  0.75 us
    reshape x1, local copies, waits for them, and re-layouts, shards(): out_bias.reshape(1, channels)  0.7 us
    reshape x1, local copies, waits for them, and re-layouts, shards(): ln_bias.reshape(1, channels)  0.7 us

profile of v1, /device:TPU:0, one launch (start us, length us, event | category | flops | bytes accessed | tf_op | source)
XLA Modules:
  0.0 23.6 jit_solution(12965051194298595194)
XLA Ops:
  0.6 0.0 copy-start.1
  0.6 0.7 %reshape.19.gain_ref = f32[1,1280]{1,0:T(1,128)S(1)} reshape(f32[1280]{0:T(1024)} %param.9) | data formatting | bytes 10240 | tf_op jit(solution)/shard_map/reshape | solution.py:288
  1.4 0.7 %reshape.20.bias_ref = f32[1,1280]{1,0:T(1,128)S(1)} reshape(f32[1280]{0:T(1024)} %param.10) | data formatting | bytes 10240 | tf_op jit(solution)/shard_map/reshape | solution.py:289
  2.1 0.7 %reshape.22.out_bias_ref = f32[1,1280]{1,0:T(1,128)S(1)} reshape(f32[1280]{0:T(1024)} %param.15) | data formatting | bytes 10240 | tf_op jit(solution)/shard_map/reshape | solution.py:294
  2.8 0.0 copy-start.2
  2.8 1.2 %copy.10.w_query_hbm = bf16[1280,64]{1,0:T(8,128)(2,1)S(1)} copy(bf16[1280,64]{0,1:T(8,128)(2,1)} %param.11) | data formatting | bytes 327680 | tf_op args[3]
  4.0 0.0 copy-done.1
  4.0 0.0 copy-done.2
  4.0 0.0 copy-start
  4.0 1.1 %copy-done = bf16[256,1280]{1,0:T(8,128)(2,1)S(1)} copy-done((bf16[256,1280]{1,0:T(8,128)(2,1)S(1)}, bf16[256,1280]{1,0:T(8,128)(2,1)}, u32[]{:S(2)}) %copy-start) | copy-done | bytes 655384
  5.1 0.0 copy-start.3
  5.1 0.8 %copy-done.3 = bf16[8,32,1,128]{3,1,2,0:T(8,128)(2,1)S(1)} copy-done((bf16[8,32,1,128]{3,1,2,0:T(8,128)(2,1)S(1)}, bf16[8,32,1,128]{3,1,2,0:T(8,128)(2,1)}, u32[]{:S(2)}) %copy-start.3) | copy-done | bytes 65560
  5.9 16.4 %shard_map.95 = (bf16[8,8,1280]{2,1,0:T(8,128)(2,1)S(1)}, bf16[8,32,128]{2,1,0:T(8,128)(2,1)S(1)}) custom-call(bf16[8,8,1280]{2,1,0:T(8,128)(2,1)S(1)} %copy-done.2, f32[1,1280]{1,0:T(1,128)S(1)} %reshape.19.gain_ref, f32[1,1280]{1,0:T(1,128)S(1)} %reshape.20.bias_ref, bf16[1280,64]{1,0:T(8,128)(2,1)S(1)} %copy.10.w_query_hbm, ...), custom_call_target="tpu_custom_call" | custom-call | tf_op jit(solution)/shard_map/pallas_call | solution.py:252
  22.3 0.7 %copy.14 = bf16[8,8,1280]{2,1,0:T(8,128)(2,1)} copy(bf16[8,8,1280]{2,1,0:T(8,128)(2,1)S(1)} %get-tuple-element.10) | data formatting | bytes 327680
  23.0 0.6 %copy.15 = bf16[8,32,1,128]{3,1,2,0:T(8,128)(2,1)} copy(bf16[8,32,1,128]{3,1,2,0:T(8,128)(2,1)S(1)} %bitcast.4) | data formatting | bytes 131072
Async XLA Ops:
  0.6 3.3 %copy-start.1 = (bf16[1280,128]{1,0:T(8,128)(2,1)S(1)}, bf16[1280,128]{1,0:T(8,128)(2,1)}, u32[]{:S(2)}) copy-start(bf16[1280,128]{1,0:T(8,128)(2,1)} %w_keyval_hbm.1) | copy-start | bytes 983044
  2.8 1.2 %copy-start.2 = (bf16[8,8,1280]{2,1,0:T(8,128)(2,1)S(1)}, bf16[8,8,1280]{2,1,0:T(8,128)(2,1)}, u32[]{:S(2)}) copy-start(bf16[8,8,1280]{2,1,0:T(8,128)(2,1)} %hidden_hbm.1) | copy-start | bytes 491524
  4.0 1.1 %copy-start = (bf16[256,1280]{1,0:T(8,128)(2,1)S(1)}, bf16[256,1280]{1,0:T(8,128)(2,1)}, u32[]{:S(2)}) copy-start(bf16[256,1280]{1,0:T(8,128)(2,1)} %w_out_hbm.1) | copy-start | bytes 1966084
  5.1 0.8 %copy-start.3 = (bf16[8,32,1,128]{3,1,2,0:T(8,128)(2,1)S(1)}, bf16[8,32,1,128]{3,1,2,0:T(8,128)(2,1)}, u32[]{:S(2)}) copy-start(bf16[8,32,1,128]{3,1,2,0:T(8,128)(2,1)} %param.13) | copy-start | bytes 196612

commit v2 on v1

--- a/solution.py
+++ b/solution.py
@@ -22,9 +22,9 @@
 
 def kernel(
     n_rows, n_cols, cores,
-    hidden_hbm, gain_ref, bias_ref, w_query_hbm, w_keyval_hbm, stale_hbm, w_out_hbm, out_bias_ref,
+    hidden_hbm, gain_hbm, bias_hbm, w_query_hbm, w_keyval_hbm, stale_hbm, w_out_hbm, out_bias_hbm,
     out_hbm, fresh_hbm,
-    hidden, w_query, w_keyval, w_out, normed, queries, keyval, fresh_wide, fresh, out, attention,
+    hidden, gain, bias, out_bias, w_query, w_keyval, w_out, normed, queries, keyval, fresh_wide, fresh, out, attention,
     load_sem, band_send, band_recv, strip_send, strip_recv, relay_send, relay_recv, att_send, att_recv, store_sem,
 ):
     row = lax.axis_index("rows")
@@ -35,7 +35,7 @@
     band_rows, strip_cols, channels = hidden.shape
     strip = band_rows * strip_cols
     pair = cores * strip
-    head_size = w_query.shape[1]
+    head_size = w_query.shape[0]
     piece = strip // PIECES
     scale = 1.0 / math.sqrt(head_size)
 
@@ -44,9 +44,12 @@
         for index, (source, target) in enumerate(
             [
                 (hidden_hbm, hidden),
+                (gain_hbm, gain),
+                (bias_hbm, bias),
                 (w_query_hbm, w_query),
                 (w_keyval_hbm, w_keyval),
                 (w_out_hbm, w_out),
+                (out_bias_hbm, out_bias),
             ]
         )
     ]
@@ -67,16 +70,6 @@
 
     repeat(n_cols - 1, greet_col)
     repeat(n_rows - 1, greet_row)
-
-    loads[0].wait()
-    values = hidden[...].astype(jnp.float32).reshape(strip, channels)
-    centred = values - jnp.mean(values, axis=-1, keepdims=True)
-    variance = jnp.mean(centred * centred, axis=-1, keepdims=True)
-    own_rows = pl.ds(pl.multiple_of(core * strip, strip), strip)
-    normed[chip, own_rows, :] = (
-        centred * lax.rsqrt(variance + 1e-05) * gain_ref[...] + bias_ref[...]
-    ).astype(jnp.bfloat16)
-    pl.semaphore_wait(barrier, n_cols - 1 + n_rows - 1)
 
     def rows_of(core_index, part):
         return pl.ds(pl.multiple_of(core_index * strip + part * piece, piece), piece)
@@ -106,16 +99,30 @@
             device_id={"rows": lax.rem(row + step + 1, n_rows)}, device_id_type=MESH,
         )
 
+    pl.semaphore_wait(barrier, n_cols - 1 + n_rows - 1)
+    repeat(n_rows - 1, lambda step: band_copy(step).start())
+
+    for load in loads[:3]:
+        load.wait()
+    gains, biases = gain[...].reshape(1, channels), bias[...].reshape(1, channels)
+    piece_rows = band_rows // PIECES
     for part in range(PIECES):
-        repeat(chips - 1, lambda step, part=part: strip_copy(step, part).start())
-    if cores > 1:
-        for part in range(PIECES):
+        values = hidden[part * piece_rows : (part + 1) * piece_rows].astype(jnp.float32)
+        values = values.reshape(piece, channels)
+        centred = values - jnp.mean(values, axis=-1, keepdims=True)
+        variance = jnp.mean(centred * centred, axis=-1, keepdims=True)
+        normed[chip, rows_of(core, part), :] = (
+            centred * lax.rsqrt(variance + 1e-05) * gains + biases
+        ).astype(jnp.bfloat16)
+        repeat(chips - 1, lambda step: strip_copy(step, part).start())
+        if cores > 1:
             relay_copy(0, part).start()
-    repeat(n_rows - 1, lambda step: band_copy(step).start())
 
     def project(index):
         rows = normed[index]
-        own = jnp.dot(rows, w_query[...], preferred_element_type=jnp.float32).astype(jnp.bfloat16)
+        own = lax.dot_general(
+            rows, w_query[...], (((1,), (1,)), ((), ())), preferred_element_type=jnp.float32
+        ).astype(jnp.bfloat16)
         queries[index] = jnp.concatenate([own, jnp.zeros_like(own)], axis=1)
         both = jnp.dot(rows, w_keyval[...], preferred_element_type=jnp.float32).astype(jnp.bfloat16)
         keyval[row, pl.ds(pl.multiple_of(index * pair, pair), pair), :] = both
@@ -123,7 +130,7 @@
         for which in range(cores):
             fresh_wide[:, index * cores + which] = wide[which]
 
-    for load in loads[1:3]:
+    for load in loads[3:5]:
         load.wait()
     if cores > 1:
         for part in range(PIECES):
@@ -214,14 +221,15 @@
         att_copy(sibling, 1).start()
     attention[1, col] = attention[0, col]
 
-    loads[3].wait()
+    for load in loads[5:]:
+        load.wait()
     if cores > 1:
         att_copy(sibling, 1).wait_recv()
     for step in range(cores, n_cols):
         att_copy(sibling, step).wait_recv()
     together_heads = jnp.concatenate([attention[1, head] for head in range(n_cols)], axis=1)
     result = jnp.dot(together_heads, w_out[...], preferred_element_type=jnp.float32)
-    result = result + out_bias_ref[...] + hidden[...].astype(jnp.float32).reshape(strip, channels)
+    result = result + out_bias[...].reshape(1, channels) + hidden[...].astype(jnp.float32).reshape(strip, channels)
     out[...] = result.reshape(out.shape).astype(jnp.bfloat16)
     out_store = pltpu.make_async_copy(out, out_hbm, store_sem.at[1])
     out_store.start()
@@ -246,8 +254,7 @@
     cores = 2 if n_cols % 2 == 0 else 1
     chips = n_cols // cores
     bf16, f32 = jnp.bfloat16, jnp.float32
-    anywhere = pl.BlockSpec(memory_space=pl.ANY)
-    near = pl.BlockSpec(memory_space=pltpu.VMEM)
+    far = pl.BlockSpec(memory_space=pltpu.HBM)
     dma = pltpu.SemaphoreType.DMA
     out, fresh = pl.pallas_call(
         functools.partial(kernel, n_rows, n_cols, cores),
@@ -255,11 +262,14 @@
             jax.ShapeDtypeStruct(hidden.shape, bf16),
             jax.ShapeDtypeStruct((band_rows, full_cols, 2 * head_size), bf16),
         ),
-        in_specs=[anywhere, near, near, anywhere, anywhere, anywhere, anywhere, near],
-        out_specs=(anywhere, anywhere),
+        in_specs=[far] * 8,
+        out_specs=(far, far),
         scratch_shapes=[
             pltpu.VMEM(hidden.shape, bf16),
-            pltpu.VMEM(w_query.shape, bf16),
+            pltpu.VMEM((channels,), f32),
+            pltpu.VMEM((channels,), f32),
+            pltpu.VMEM((channels,), f32),
+            pltpu.VMEM((head_size, channels), bf16),
             pltpu.VMEM(w_keyval.shape, bf16),
             pltpu.VMEM(w_out.shape, bf16),
             pltpu.VMEM((chips, cores * strip, channels), bf16),
@@ -269,7 +279,7 @@
             pltpu.VMEM((band_rows, full_cols, 2 * head_size), bf16),
             pltpu.VMEM(hidden.shape, bf16),
             pltpu.VMEM((2, n_cols, strip, head_size), bf16),
-            dma((4,)),
+            dma((7,)),
             dma((n_rows,)),
             dma((n_rows,)),
             dma((chips, PIECES)),
@@ -281,17 +291,17 @@
             dma((2,)),
         ],
         compiler_params=pltpu.CompilerParams(
-            collective_id=0, has_side_effects=True, vmem_limit_bytes=48 * 1024 * 1024
+            collective_id=0, has_side_effects=True, vmem_limit_bytes=64 * 1024 * 1024
         ),
     )(
         hidden,
-        ln_gain.reshape(1, channels),
-        ln_bias.reshape(1, channels),
-        w_query,
+        ln_gain,
+        ln_bias,
+        w_query.T,
         w_keyval,
         stale_keyval.reshape(cells, 2 * head_size),
         w_out,
-        out_bias.reshape(1, channels),
+        out_bias,
     )
     return out, fresh.reshape(band_rows, full_cols, 1, 2 * head_size)
 

time: 24 us -> 19.5 us (0.81)
  local copies, waits for them, and re-layouts: 6.55 us -> 2.26 us
    reshape x3 -> x0, local copies, waits for them, and re-layouts: 2.15 us -> none  [the longest x1 0.75 us: shards(): ln_gain.reshape(1, channels)]
    unnamed x11 -> x4, local copies, waits for them, and re-layouts: 4.4 us -> 2.26 us
where the time goes in v2:
time: 19.5 us; the launch traced here: 19.3 us
  Pallas kernels  16.4 us (84%)
  local copies, waits for them, and re-layouts  2.26 us (12%)
  between operations  0.65 us (3%)
    pallas_call x1, Pallas kernels, shards(): pl.pallas_call(functools.partial(kernel, n_rows, n_cols, cores), out_shap...  16.4 us
    unnamed x4, local copies, waits for them, and re-layouts  2.26 us

profile of v2, /device:TPU:0, one launch (start us, length us, event | category | flops | bytes accessed | tf_op | source)
XLA Modules:
  0.0 19.3 jit_solution(9374816536980555666)
XLA Ops:
  0.6 16.4 %shard_map.95 = (bf16[8,8,1280]{2,1,0:T(8,128)(2,1)}, bf16[8,32,128]{2,1,0:T(8,128)(2,1)}) custom-call(bf16[8,8,1280]{2,1,0:T(8,128)(2,1)} %hidden_hbm.1, f32[1280]{0:T(1024)} %gain_hbm.1, f32[1280]{0:T(1024)} %bias_hbm.1, bf16[64,1280]{1,0:T(8,128)(2,1)} %bitcast.5, bf16[1280,128]{1,0:T(8,128)(2,1)} %w_keyval_hbm.1, bf16[256,128]{1,0:T(8,128)(2,1)} %bitcast.6, ...), custom_call_target="tpu_custom_call" | custom-call | tf_op jit(solution)/shard_map/pallas_call | solution.py:259
  17.1 0.0 copy-start
  17.1 1.6 %copy.13 = bf16[8,8,1280]{2,1,0:T(8,128)(2,1)} copy(bf16[8,8,1280]{2,1,0:T(8,128)(2,1)} %get-tuple-element.10) | data formatting | bytes 327680
  18.7 0.0 copy-done
  18.7 0.6 %copy.14 = bf16[8,32,1,128]{3,1,2,0:T(8,128)(2,1)} copy(bf16[8,32,1,128]{3,1,2,0:T(8,128)(2,1)S(1)} %bitcast.7) | data formatting | bytes 131072
Async XLA Ops:
  17.1 1.6 %copy-start = (bf16[8,32,128]{2,1,0:T(8,128)(2,1)S(1)}, bf16[8,32,128]{2,1,0:T(8,128)(2,1)}, u32[]{:S(2)}) copy-start(bf16[8,32,128]{2,1,0:T(8,128)(2,1)} %get-tuple-element.5) | copy-start | bytes 196612

commit v3 on v2

--- a/solution.py
+++ b/solution.py
@@ -23,9 +23,9 @@
 def kernel(
     n_rows, n_cols, cores,
     hidden_hbm, gain_hbm, bias_hbm, w_query_hbm, w_keyval_hbm, stale_hbm, w_out_hbm, out_bias_hbm,
-    out_hbm, fresh_hbm,
-    hidden, gain, bias, out_bias, w_query, w_keyval, w_out, normed, queries, keyval, fresh_wide, fresh, out, attention,
-    load_sem, band_send, band_recv, strip_send, strip_recv, relay_send, relay_recv, att_send, att_recv, store_sem,
+    out, fresh,
+    hidden, gain, bias, out_bias, w_query, w_keyval, w_out, normed, queries, keyval, fresh_wide, attention,
+    load_sem, band_send, band_recv, strip_send, strip_recv, relay_send, relay_recv, att_send, att_recv,
 ):
     row = lax.axis_index("rows")
     col = lax.axis_index("cols")
@@ -150,8 +150,6 @@
     repeat(chips - 1, arrive)
 
     fresh[...] = fresh_wide[...].reshape(fresh.shape).astype(jnp.bfloat16)
-    fresh_store = pltpu.make_async_copy(fresh, fresh_hbm, store_sem.at[0])
-    fresh_store.start()
 
     repeat(n_rows - 1, lambda step: band_copy(step).wait_recv())
 
@@ -231,8 +229,6 @@
     result = jnp.dot(together_heads, w_out[...], preferred_element_type=jnp.float32)
     result = result + out_bias[...].reshape(1, channels) + hidden[...].astype(jnp.float32).reshape(strip, channels)
     out[...] = result.reshape(out.shape).astype(jnp.bfloat16)
-    out_store = pltpu.make_async_copy(out, out_hbm, store_sem.at[1])
-    out_store.start()
 
     for part in range(PIECES):
         repeat(chips - 1, lambda step, part=part: strip_copy(step, part).wait_send())
@@ -241,8 +237,17 @@
     repeat(n_rows - 1, lambda step: band_copy(step).wait_send())
     for step in range(1, n_cols):
         att_copy(sibling, step).wait_send()
-    fresh_store.wait()
-    out_store.wait()
+
+
+def write_back(out, fresh, out_hbm, fresh_hbm, store_sem):
+    stores = [
+        pltpu.make_async_copy(out, out_hbm, store_sem.at[0]),
+        pltpu.make_async_copy(fresh, fresh_hbm, store_sem.at[1]),
+    ]
+    for store in stores:
+        store.start()
+    for store in stores:
+        store.wait()
 
 
 def shards(n_rows, n_cols, hidden, ln_gain, ln_bias, w_query, w_keyval, stale_keyval, w_out, out_bias):
@@ -254,16 +259,25 @@
     cores = 2 if n_cols % 2 == 0 else 1
     chips = n_cols // cores
     bf16, f32 = jnp.bfloat16, jnp.float32
+    near = pl.BlockSpec(memory_space=pltpu.VMEM)
     far = pl.BlockSpec(memory_space=pltpu.HBM)
     dma = pltpu.SemaphoreType.DMA
-    out, fresh = pl.pallas_call(
+    operands = (
+        hidden,
+        ln_gain,
+        ln_bias,
+        w_query.T,
+        w_keyval,
+        stale_keyval.reshape(cells, 2 * head_size),
+        w_out,
+        out_bias,
+    )
+    shapes = (hidden.shape, (band_rows, full_cols, 2 * head_size))
+    found = pl.pallas_call(
         functools.partial(kernel, n_rows, n_cols, cores),
-        out_shape=(
-            jax.ShapeDtypeStruct(hidden.shape, bf16),
-            jax.ShapeDtypeStruct((band_rows, full_cols, 2 * head_size), bf16),
-        ),
+        out_shape=tuple(pltpu.VMEM(shape, bf16) for shape in shapes),
         in_specs=[far] * 8,
-        out_specs=(far, far),
+        out_specs=(near, near),
         scratch_shapes=[
             pltpu.VMEM(hidden.shape, bf16),
             pltpu.VMEM((channels,), f32),
@@ -276,8 +290,6 @@
             pltpu.VMEM((chips, cores * strip, 2 * head_size), bf16),
             pltpu.VMEM((n_rows, cells, 2 * head_size), bf16),
             pltpu.VMEM((band_rows, n_cols, strip_cols, 2 * head_size), f32),
-            pltpu.VMEM((band_rows, full_cols, 2 * head_size), bf16),
-            pltpu.VMEM(hidden.shape, bf16),
             pltpu.VMEM((2, n_cols, strip, head_size), bf16),
             dma((7,)),
             dma((n_rows,)),
@@ -288,21 +300,18 @@
             dma((chips, PIECES)),
             dma((n_cols,)),
             dma((n_cols,)),
-            dma((2,)),
         ],
         compiler_params=pltpu.CompilerParams(
-            collective_id=0, has_side_effects=True, vmem_limit_bytes=64 * 1024 * 1024
+            collective_id=0, has_side_effects=True, vmem_limit_bytes=48 * 1024 * 1024
         ),
-    )(
-        hidden,
-        ln_gain,
-        ln_bias,
-        w_query.T,
-        w_keyval,
-        stale_keyval.reshape(cells, 2 * head_size),
-        w_out,
-        out_bias,
-    )
+    )(*(pltpu.with_memory_space_constraint(operand, pltpu.HBM) for operand in operands))
+    out, fresh = pl.pallas_call(
+        write_back,
+        out_shape=tuple(pltpu.HBM(shape, bf16) for shape in shapes),
+        in_specs=[near, near],
+        out_specs=(far, far),
+        scratch_shapes=[dma((2,))],
+    )(*found)
     return out, fresh.reshape(band_rows, full_cols, 1, 2 * head_size)
 
 

time: 19.5 us -> 19.5 us (level)
  Pallas kernels: 16.4 us -> 17.4 us
  local copies, waits for them, and re-layouts: 2.26 us -> 1.27 us
    pallas_call x0 -> x1, Pallas kernels: none -> 1.62 us  [shards(): pl.pallas_call(write_back, out_shape=tuple((pltpu.HBM(shape, bf16) for sh...]
    unnamed x4, local copies, waits for them, and re-layouts: 2.26 us -> 1.27 us
    pallas_call x1, Pallas kernels: 16.4 us -> 15.8 us  [shards(): pl.pallas_call(functools.partial(kernel, n_rows, n_cols, cores), out_shap...]
where the time goes in v3:
time: 19.5 us; the launch traced here: 19.3 us
  Pallas kernels  17.4 us (89%)
  local copies, waits for them, and re-layouts  1.27 us (7%)
  between operations  0.65 us (3%)
    pallas_call x1, Pallas kernels, shards(): pl.pallas_call(functools.partial(kernel, n_rows, n_cols, cores), out_shap...  15.8 us
    pallas_call x1, Pallas kernels, shards(): pl.pallas_call(write_back, out_shape=tuple((pltpu.HBM(shape, bf16) for sh...  1.62 us
    unnamed x4, local copies, waits for them, and re-layouts  1.27 us

profile of v3, /device:TPU:0, one launch (start us, length us, event | category | flops | bytes accessed | tf_op | source)
XLA Modules:
  0.0 19.3 jit_solution(5523290081549927787)
XLA Ops:
  0.6 15.8 %shard_map.95 = (bf16[8,8,1280]{2,1,0:T(8,128)(2,1)S(1)}, bf16[8,32,128]{2,1,0:T(8,128)(2,1)S(1)}) custom-call(bf16[8,8,1280]{2,1,0:T(8,128)(2,1)} %hidden_hbm.1, f32[1280]{0:T(1024)} %gain_hbm.1, f32[1280]{0:T(1024)} %bias_hbm.1, bf16[64,1280]{1,0:T(8,128)(2,1)} %bitcast.5, bf16[1280,128]{1,0:T(8,128)(2,1)} %w_keyval_hbm.1, bf16[256,128]{1,0:T(8,128)(2,1)} %bitcast.6, ...), custom_call_target="tpu_custom_call" | custom-call | tf_op jit(solution)/shard_map/pallas_call | solution.py:276
  16.4 0.0 copy-start
  16.4 0.6 %copy-done = bf16[8,8,1280]{2,1,0:T(8,128)(2,1)} copy-done((bf16[8,8,1280]{2,1,0:T(8,128)(2,1)}, bf16[8,8,1280]{2,1,0:T(8,128)(2,1)S(1)}, u32[]{:S(2)}) %copy-start) | copy-done | bytes 163864
  17.1 0.0 copy-start.1
  17.1 0.6 %copy-done.1 = bf16[8,32,128]{2,1,0:T(8,128)(2,1)} copy-done((bf16[8,32,128]{2,1,0:T(8,128)(2,1)}, bf16[8,32,128]{2,1,0:T(8,128)(2,1)S(1)}, u32[]{:S(2)}) %copy-start.1) | copy-done | bytes 65560
  17.7 1.6 %shard_map.96 = (bf16[8,8,1280]{2,1,0:T(8,128)(2,1)}, bf16[8,32,128]{2,1,0:T(8,128)(2,1)}) custom-call(bf16[8,8,1280]{2,1,0:T(8,128)(2,1)} %copy-done, bf16[8,32,128]{2,1,0:T(8,128)(2,1)} %copy-done.1), custom_call_target="tpu_custom_call" | custom-call | tf_op jit(solution)/shard_map/pallas_call | solution.py:308
Async XLA Ops:
  16.4 0.7 %copy-start = (bf16[8,8,1280]{2,1,0:T(8,128)(2,1)}, bf16[8,8,1280]{2,1,0:T(8,128)(2,1)S(1)}, u32[]{:S(2)}) copy-start(bf16[8,8,1280]{2,1,0:T(8,128)(2,1)S(1)} %get-tuple-element.6.out) | copy-start | bytes 491524
  17.1 0.6 %copy-start.1 = (bf16[8,32,128]{2,1,0:T(8,128)(2,1)}, bf16[8,32,128]{2,1,0:T(8,128)(2,1)S(1)}, u32[]{:S(2)}) copy-start(bf16[8,32,128]{2,1,0:T(8,128)(2,1)S(1)} %get-tuple-element.7.fresh) | copy-start | bytes 196612

commit v4 on v3

--- a/solution.py
+++ b/solution.py
@@ -10,6 +10,7 @@
 
 MESH = pl.DeviceIdType.MESH
 PIECES = 4
+HALVES = 2
 
 
 def repeat(count, body):
@@ -25,7 +26,7 @@
     hidden_hbm, gain_hbm, bias_hbm, w_query_hbm, w_keyval_hbm, stale_hbm, w_out_hbm, out_bias_hbm,
     out, fresh,
     hidden, gain, bias, out_bias, w_query, w_keyval, w_out, normed, queries, keyval, fresh_wide, attention,
-    load_sem, band_send, band_recv, strip_send, strip_recv, relay_send, relay_recv, att_send, att_recv,
+    load_sem, right_send, right_recv, left_send, left_recv, strip_send, strip_recv, relay_send, relay_recv, att_send, att_recv,
 ):
     row = lax.axis_index("rows")
     col = lax.axis_index("cols")
@@ -63,13 +64,13 @@
             barrier, inc=1, device_id={"cols": lax.rem(col + step + 1, n_cols)}, device_id_type=MESH
         )
 
-    def greet_row(step):
-        pl.semaphore_signal(
-            barrier, inc=1, device_id={"rows": lax.rem(row + step + 1, n_rows)}, device_id_type=MESH
-        )
-
+    def greet_row(other):
+        pl.semaphore_signal(barrier, inc=1, device_id={"rows": other}, device_id_type=MESH)
+
+    has_left, has_right = row >= 1, row + 1 < n_rows
+    pl.when(has_left)(lambda: greet_row(row - 1))
+    pl.when(has_right)(lambda: greet_row(row + 1))
     repeat(n_cols - 1, greet_col)
-    repeat(n_rows - 1, greet_row)
 
     def rows_of(core_index, part):
         return pl.ds(pl.multiple_of(core_index * strip + part * piece, piece), piece)
@@ -92,15 +93,50 @@
             device_id={"cols": sibling}, device_id_type=MESH,
         )
 
-    def band_copy(step):
-        return pltpu.make_async_remote_copy(
-            src_ref=stale_hbm, dst_ref=keyval.at[row],
-            send_sem=band_send.at[step], recv_sem=band_recv.at[step],
-            device_id={"rows": lax.rem(row + step + 1, n_rows)}, device_id_type=MESH,
-        )
-
-    pl.semaphore_wait(barrier, n_cols - 1 + n_rows - 1)
-    repeat(n_rows - 1, lambda step: band_copy(step).start())
+    half_cells = keyval.shape[1] // HALVES
+
+    def right_copy(distance, half):
+        place = pl.ds(half * half_cells, half_cells)
+        source = stale_hbm.at[place] if isinstance(distance, int) and distance == 0 else keyval.at[row - distance, place]
+        return pltpu.make_async_remote_copy(
+            src_ref=source, dst_ref=keyval.at[row - distance, place],
+            send_sem=right_send.at[distance, half], recv_sem=right_recv.at[distance, half],
+            device_id={"rows": lax.rem(row + 1, n_rows)}, device_id_type=MESH,
+        )
+
+    def left_copy(distance, half):
+        place = pl.ds(half * half_cells, half_cells)
+        source = stale_hbm.at[place] if isinstance(distance, int) and distance == 0 else keyval.at[row + distance, place]
+        return pltpu.make_async_remote_copy(
+            src_ref=source, dst_ref=keyval.at[row + distance, place],
+            send_sem=left_send.at[distance, half], recv_sem=left_recv.at[distance, half],
+            device_id={"rows": lax.rem(row + n_rows - 1, n_rows)}, device_id_type=MESH,
+        )
+
+    def arrived(recv_sem, source, distance, half):
+        block = keyval.at[source, pl.ds(half * half_cells, half_cells)]
+        pltpu.make_async_copy(block, block, recv_sem.at[distance - 1, half]).wait()
+
+    def hand_on(distance, half):
+        @pl.when(row >= distance)
+        def from_left():
+            arrived(right_recv, row - distance, distance, half)
+            pl.when(has_right)(lambda: right_copy(distance, half).start())
+
+        @pl.when(row + distance < n_rows)
+        def from_right():
+            arrived(left_recv, row + distance, distance, half)
+            pl.when(has_left)(lambda: left_copy(distance, half).start())
+
+    def handed_on(distance, half):
+        pl.when((row >= distance) & has_right)(lambda: right_copy(distance, half).wait_send())
+        pl.when((row + distance < n_rows) & has_left)(lambda: left_copy(distance, half).wait_send())
+
+    neighbours = has_left.astype(jnp.int32) + has_right.astype(jnp.int32)
+    pl.semaphore_wait(barrier, n_cols - 1 + neighbours)
+    for half in range(HALVES):
+        pl.when(has_right)(lambda half=half: right_copy(0, half).start())
+        pl.when(has_left)(lambda half=half: left_copy(0, half).start())
 
     for load in loads[:3]:
         load.wait()
@@ -137,8 +173,16 @@
             relay_copy(0, part).wait_recv()
     project(chip)
 
+    few = n_rows <= 4
+    if few:
+        pending = [(distance, half) for distance in range(1, n_rows) for half in range(HALVES)]
+    else:
+        pending = []
+
     def arrive(step):
         for part in range(PIECES):
+            if pending and pending[0][0] < n_rows - 1:
+                hand_on(*pending.pop(0))
             strip_copy(step, part).wait_recv()
             if cores > 1:
                 relay_copy(step + 1, part).start()
@@ -147,11 +191,18 @@
                 relay_copy(step + 1, part).wait_recv()
         project(lax.rem(chip + chips - step - 1, chips))
 
+    if not few:
+
+        @pl.loop(1, n_rows)
+        def hand_all_on(distance):
+            for half in range(HALVES):
+                hand_on(distance, half)
+
     repeat(chips - 1, arrive)
+    for distance, half in pending:
+        hand_on(distance, half)
 
     fresh[...] = fresh_wide[...].reshape(fresh.shape).astype(jnp.bfloat16)
-
-    repeat(n_rows - 1, lambda step: band_copy(step).wait_recv())
 
     cells = keyval.shape[1]
     together = max(size for size in range(1, n_rows + 1) if n_rows % size == 0 and (size == 1 or size * cells <= 1024))
@@ -234,7 +285,13 @@
         repeat(chips - 1, lambda step, part=part: strip_copy(step, part).wait_send())
         if cores > 1:
             repeat(chips, lambda step, part=part: relay_copy(step, part).wait_send())
-    repeat(n_rows - 1, lambda step: band_copy(step).wait_send())
+    for half in range(HALVES):
+        handed_on(0, half)
+        if few:
+            for distance in range(1, n_rows - 1):
+                handed_on(distance, half)
+        else:
+            pl.loop(1, n_rows - 1)(lambda distance, half=half: handed_on(distance, half))
     for step in range(1, n_cols):
         att_copy(sibling, step).wait_send()
 
@@ -292,8 +349,10 @@
             pltpu.VMEM((band_rows, n_cols, strip_cols, 2 * head_size), f32),
             pltpu.VMEM((2, n_cols, strip, head_size), bf16),
             dma((7,)),
-            dma((n_rows,)),
-            dma((n_rows,)),
+            dma((n_rows, HALVES)),
+            dma((n_rows, HALVES)),
+            dma((n_rows, HALVES)),
+            dma((n_rows, HALVES)),
             dma((chips, PIECES)),
             dma((chips, PIECES)),
             dma((chips, PIECES)),
@@ -308,9 +367,10 @@
     out, fresh = pl.pallas_call(
         write_back,
         out_shape=tuple(pltpu.HBM(shape, bf16) for shape in shapes),
-        in_specs=[near, near],
+        in_specs=[pl.BlockSpec(memory_space=pl.ANY)] * 2,
         out_specs=(far, far),
         scratch_shapes=[dma((2,))],
+        compiler_params=pltpu.CompilerParams(vmem_limit_bytes=2 * 1024 * 1024),
     )(*found)
     return out, fresh.reshape(band_rows, full_cols, 1, 2 * head_size)
 

time: 19.5 us -> 19.5 us (level)
  Pallas kernels: 17.4 us -> 18.7 us
  local copies, waits for them, and re-layouts: 1.27 us -> 0 us
    pallas_call x1, Pallas kernels: 15.8 us -> 18 us  [shards(): pl.pallas_call(functools.partial(kernel, n_rows, n_cols, cores), out_shap...]
    unnamed x4 -> x0, local copies, waits for them, and re-layouts: 1.27 us -> none
    pallas_call x1, Pallas kernels: 1.62 us -> 0.7 us  [shards(): pl.pallas_call(write_back, out_shape=tuple((pltpu.HBM(shape, bf16) for sh...]
where the time goes in v4:
time: 19.5 us; the launch traced here: 19.4 us
  Pallas kernels  18.7 us (96%)
  between operations  0.64 us (3%)
    pallas_call x1, Pallas kernels, shards(): pl.pallas_call(functools.partial(kernel, n_rows, n_cols, cores), out_shap...  18 us
    pallas_call x1, Pallas kernels, shards(): pl.pallas_call(write_back, out_shape=tuple((pltpu.HBM(shape, bf16) for sh...  0.7 us

profile of v4, /device:TPU:0, one launch (start us, length us, event | category | flops | bytes accessed | tf_op | source)
XLA Modules:
  0.0 19.4 jit_solution(8673932433959886296)
XLA Ops:
  0.6 18.0 %shard_map.95 = (bf16[8,8,1280]{2,1,0:T(8,128)(2,1)S(1)}, bf16[8,32,128]{2,1,0:T(8,128)(2,1)S(1)}) custom-call(bf16[8,8,1280]{2,1,0:T(8,128)(2,1)} %hidden_hbm.1, f32[1280]{0:T(1024)} %gain_hbm.1, f32[1280]{0:T(1024)} %bias_hbm.1, bf16[64,1280]{1,0:T(8,128)(2,1)} %bitcast.5, bf16[1280,128]{1,0:T(8,128)(2,1)} %w_keyval_hbm.1, bf16[256,128]{1,0:T(8,128)(2,1)} %bitcast.6, ...), custom_call_target="tpu_custom_call" | custom-call | tf_op jit(solution)/shard_map/pallas_call | solution.py:333
  18.7 0.7 %shard_map.96 = (bf16[8,8,1280]{2,1,0:T(8,128)(2,1)}, bf16[8,32,128]{2,1,0:T(8,128)(2,1)}) custom-call(bf16[8,8,1280]{2,1,0:T(8,128)(2,1)S(1)} %get-tuple-element.6.out, bf16[8,32,128]{2,1,0:T(8,128)(2,1)S(1)} %get-tuple-element.7.fresh), custom_call_target="tpu_custom_call" | custom-call | tf_op jit(solution)/shard_map/pallas_call | solution.py:367

commit v5 on v3

--- a/solution.py
+++ b/solution.py
@@ -37,7 +37,7 @@
     pair = cores * strip
     head_size = w_query.shape[0]
     piece = strip // PIECES
-    scale = 1.0 / math.sqrt(head_size)
+    scale = math.log2(math.e) / math.sqrt(head_size)
 
     loads = [
         pltpu.make_async_copy(source, target, load_sem.at[index])
@@ -92,15 +92,26 @@
             device_id={"cols": sibling}, device_id_type=MESH,
         )
 
-    def band_copy(step):
+    def by_distance(step):
+        tables = [sorted(range(n_rows), key=lambda band: (abs(band - at), band))[step] for at in range(n_rows)]
+        band = tables[0]
+        for at in range(1, n_rows):
+            band = jnp.where(row == at, tables[at], band)
+        return band
+
+    def band_copy(target):
         return pltpu.make_async_remote_copy(
             src_ref=stale_hbm, dst_ref=keyval.at[row],
-            send_sem=band_send.at[step], recv_sem=band_recv.at[step],
-            device_id={"rows": lax.rem(row + step + 1, n_rows)}, device_id_type=MESH,
-        )
+            send_sem=band_send.at[target], recv_sem=band_recv.at[row],
+            device_id={"rows": target}, device_id_type=MESH,
+        )
+
+    def band_arrived(band):
+        pltpu.make_async_copy(keyval.at[band], keyval.at[band], band_recv.at[band]).wait()
 
     pl.semaphore_wait(barrier, n_cols - 1 + n_rows - 1)
-    repeat(n_rows - 1, lambda step: band_copy(step).start())
+    for step in range(1, n_rows):
+        band_copy(by_distance(step)).start()
 
     for load in loads[:3]:
         load.wait()
@@ -151,48 +162,45 @@
 
     fresh[...] = fresh_wide[...].reshape(fresh.shape).astype(jnp.bfloat16)
 
-    repeat(n_rows - 1, lambda step: band_copy(step).wait_recv())
-
-    cells = keyval.shape[1]
-    together = max(size for size in range(1, n_rows + 1) if n_rows % size == 0 and (size == 1 or size * cells <= 1024))
-
-    def absorb(own, index):
-        block = keyval[pl.ds(index * together, together)].reshape(together * cells, keyval.shape[2])
+    def absorb(state, own, band):
+        block = keyval[band]
         scores = lax.dot_general(
             own, block, (((1,), (1,)), ((), ())), preferred_element_type=jnp.float32
         )
-        return block, scores
-
-    def attend(index):
-        own = queries[index]
-        if together == n_rows:
-            block, scores = absorb(own, 0)
-            row_max = jnp.max(scores, axis=-1, keepdims=True)
-            weights = jnp.exp((scores - row_max) * scale)
-            denominator = jnp.sum(weights, axis=-1, keepdims=True)
-            weighted = jnp.dot(weights.astype(jnp.bfloat16), block, preferred_element_type=jnp.float32)
-        else:
-
-            def body(step, state):
-                row_max, denominator, weighted = state
-                block, scores = absorb(own, step)
-                new_max = jnp.maximum(row_max, jnp.max(scores, axis=-1, keepdims=True))
-                factor = jnp.exp((row_max - new_max) * scale)
-                weights = jnp.exp((scores - new_max) * scale)
-                return (
-                    new_max,
-                    denominator * factor + jnp.sum(weights, axis=-1, keepdims=True),
-                    weighted * factor
-                    + jnp.dot(weights.astype(jnp.bfloat16), block, preferred_element_type=jnp.float32),
-                )
-
-            initial = (
-                jnp.full((pair, 1), -1e30, jnp.float32),
-                jnp.zeros((pair, 1), jnp.float32),
-                jnp.zeros((pair, 2 * head_size), jnp.float32),
-            )
-            row_max, denominator, weighted = lax.fori_loop(0, n_rows // together, body, initial)
-        return (weighted[:, head_size:] / denominator).astype(jnp.bfloat16)
+        new_max = jnp.max(scores, axis=-1, keepdims=True)
+        if state is not None:
+            new_max = jnp.maximum(state[0], new_max)
+        weights = jnp.exp2((scores - new_max) * scale)
+        denominator = jnp.sum(weights, axis=-1, keepdims=True)
+        weighted = jnp.dot(weights.astype(jnp.bfloat16), block, preferred_element_type=jnp.float32)
+        if state is not None:
+            factor = jnp.exp2((state[0] - new_max) * scale)
+            denominator = state[1] * factor + denominator
+            weighted = state[2] * factor + weighted
+        return new_max, denominator, weighted
+
+    def keep(state, first, count):
+        found = (state[2][:, head_size:] / state[1]).astype(jnp.bfloat16)
+        for which in range(count):
+            attention[0, first + which] = found[which * strip : (which + 1) * strip]
+
+    if n_rows * chips <= 16:
+        own = queries[...].reshape(n_cols * strip, queries.shape[2])
+        state = absorb(None, own, row)
+        for step in range(1, n_rows):
+            band = by_distance(step)
+            band_arrived(band)
+            state = absorb(state, own, band)
+        keep(state, 0, n_cols)
+    else:
+        for step in range(1, n_rows):
+            band_arrived(by_distance(step))
+
+        @pl.loop(0, chips)
+        def each_pair(index):
+            own = queries[index]
+            state = lax.fori_loop(1, n_rows, lambda band, state: absorb(state, own, band), absorb(None, own, 0))
+            keep(state, index * cores, cores)
 
     def att_copy(target, step):
         return pltpu.make_async_remote_copy(
@@ -203,18 +211,11 @@
 
     def serve(step):
         other = lax.rem(chip + step + 1, chips)
-        found = attend(other)
-        for which in range(cores):
-            target = other * cores + lax.rem(core + which, cores)
-            attention[0, other * cores + which] = found[which * strip : (which + 1) * strip]
         for which in range(cores):
             target = other * cores + lax.rem(core + which, cores)
             att_copy(target, (step + 1) * cores + which).start()
 
     repeat(chips - 1, serve)
-    found = attend(chip)
-    for which in range(cores):
-        attention[0, chip * cores + which] = found[which * strip : (which + 1) * strip]
     if cores > 1:
         att_copy(sibling, 1).start()
     attention[1, col] = attention[0, col]
@@ -234,7 +235,8 @@
         repeat(chips - 1, lambda step, part=part: strip_copy(step, part).wait_send())
         if cores > 1:
             repeat(chips, lambda step, part=part: relay_copy(step, part).wait_send())
-    repeat(n_rows - 1, lambda step: band_copy(step).wait_send())
+    for step in range(1, n_rows):
+        band_copy(by_distance(step)).wait_send()
     for step in range(1, n_cols):
         att_copy(sibling, step).wait_send()
 
@@ -308,9 +310,10 @@
     out, fresh = pl.pallas_call(
         write_back,
         out_shape=tuple(pltpu.HBM(shape, bf16) for shape in shapes),
-        in_specs=[near, near],
+        in_specs=[pl.BlockSpec(memory_space=pl.ANY)] * 2,
         out_specs=(far, far),
         scratch_shapes=[dma((2,))],
+        compiler_params=pltpu.CompilerParams(vmem_limit_bytes=2 * 1024 * 1024),
     )(*found)
     return out, fresh.reshape(band_rows, full_cols, 1, 2 * head_size)
 

time: 19.5 us -> 18.4 us (0.944)
  local copies, waits for them, and re-layouts: 1.27 us -> 0 us
  Pallas kernels: 17.4 us -> 17.6 us
    unnamed x4 -> x0, local copies, waits for them, and re-layouts: 1.27 us -> none
    pallas_call x1, Pallas kernels: 15.8 us -> 16.9 us  [shards(): pl.pallas_call(functools.partial(kernel, n_rows, n_cols, cores), out_shap...]
    pallas_call x1, Pallas kernels: 1.62 us -> 0.7 us  [shards(): pl.pallas_call(write_back, out_shape=tuple((pltpu.HBM(shape, bf16) for sh...]
where the time goes in v5:
time: 18.4 us; the launch traced here: 18.2 us
  Pallas kernels  17.6 us (96%)
  between operations  0.64 us (3%)
    pallas_call x1, Pallas kernels, shards(): pl.pallas_call(functools.partial(kernel, n_rows, n_cols, cores), out_shap...  16.9 us
    pallas_call x1, Pallas kernels, shards(): pl.pallas_call(write_back, out_shape=tuple((pltpu.HBM(shape, bf16) for sh...  0.7 us

profile of v5, /device:TPU:0, one launch (start us, length us, event | category | flops | bytes accessed | tf_op | source)
XLA Modules:
  0.0 18.2 jit_solution(2242364394409157104)
XLA Ops:
  0.6 16.9 %shard_map.95 = (bf16[8,8,1280]{2,1,0:T(8,128)(2,1)S(1)}, bf16[8,32,128]{2,1,0:T(8,128)(2,1)S(1)}) custom-call(bf16[8,8,1280]{2,1,0:T(8,128)(2,1)} %hidden_hbm.1, f32[1280]{0:T(1024)} %gain_hbm.1, f32[1280]{0:T(1024)} %bias_hbm.1, bf16[64,1280]{1,0:T(8,128)(2,1)} %bitcast.5, bf16[1280,128]{1,0:T(8,128)(2,1)} %w_keyval_hbm.1, bf16[256,128]{1,0:T(8,128)(2,1)} %bitcast.6, ...), custom_call_target="tpu_custom_call" | custom-call | tf_op jit(solution)/shard_map/pallas_call | solution.py:278
  17.5 0.7 %shard_map.96 = (bf16[8,8,1280]{2,1,0:T(8,128)(2,1)}, bf16[8,32,128]{2,1,0:T(8,128)(2,1)}) custom-call(bf16[8,8,1280]{2,1,0:T(8,128)(2,1)S(1)} %get-tuple-element.6.out, bf16[8,32,128]{2,1,0:T(8,128)(2,1)S(1)} %get-tuple-element.7.fresh), custom_call_target="tpu_custom_call" | custom-call | tf_op jit(solution)/shard_map/pallas_call | solution.py:310

commit v6 on v5

--- a/solution.py
+++ b/solution.py
@@ -165,14 +165,15 @@
     def absorb(state, own, band):
         block = keyval[band]
         scores = lax.dot_general(
-            own, block, (((1,), (1,)), ((), ())), preferred_element_type=jnp.float32
-        )
-        new_max = jnp.max(scores, axis=-1, keepdims=True)
+            block, own, (((1,), (1,)), ((), ())), preferred_element_type=jnp.float32
+        )
+        block_values = block.T[head_size:]
+        new_max = jnp.max(scores, axis=0, keepdims=True)
         if state is not None:
             new_max = jnp.maximum(state[0], new_max)
         weights = jnp.exp2((scores - new_max) * scale)
-        denominator = jnp.sum(weights, axis=-1, keepdims=True)
-        weighted = jnp.dot(weights.astype(jnp.bfloat16), block, preferred_element_type=jnp.float32)
+        denominator = jnp.sum(weights, axis=0, keepdims=True)
+        weighted = jnp.dot(block_values, weights.astype(jnp.bfloat16), preferred_element_type=jnp.float32)
         if state is not None:
             factor = jnp.exp2((state[0] - new_max) * scale)
             denominator = state[1] * factor + denominator
@@ -180,7 +181,7 @@
         return new_max, denominator, weighted
 
     def keep(state, first, count):
-        found = (state[2][:, head_size:] / state[1]).astype(jnp.bfloat16)
+        found = (state[2] / state[1]).T.astype(jnp.bfloat16)
         for which in range(count):
             attention[0, first + which] = found[which * strip : (which + 1) * strip]
 

time: 18.4 us -> 18.4 us (level)
  no operation moved by 1% of the time
where the time goes in v6:
time: 18.4 us; the launch traced here: 18.2 us
  Pallas kernels  17.6 us (96%)
  between operations  0.64 us (3%)
    pallas_call x1, Pallas kernels, shards(): pl.pallas_call(functools.partial(kernel, n_rows, n_cols, cores), out_shap...  16.9 us
    pallas_call x1, Pallas kernels, shards(): pl.pallas_call(write_back, out_shape=tuple((pltpu.HBM(shape, bf16) for sh...  0.7 us

profile of v6, /device:TPU:0, one launch (start us, length us, event | category | flops | bytes accessed | tf_op | source)
XLA Modules:
  0.0 18.2 jit_solution(17311293850957003782)
XLA Ops:
  0.6 16.9 %shard_map.95 = (bf16[8,8,1280]{2,1,0:T(8,128)(2,1)S(1)}, bf16[8,32,128]{2,1,0:T(8,128)(2,1)S(1)}) custom-call(bf16[8,8,1280]{2,1,0:T(8,128)(2,1)} %hidden_hbm.1, f32[1280]{0:T(1024)} %gain_hbm.1, f32[1280]{0:T(1024)} %bias_hbm.1, bf16[64,1280]{1,0:T(8,128)(2,1)} %bitcast.5, bf16[1280,128]{1,0:T(8,128)(2,1)} %w_keyval_hbm.1, bf16[256,128]{1,0:T(8,128)(2,1)} %bitcast.6, ...), custom_call_target="tpu_custom_call" | custom-call | tf_op jit(solution)/shard_map/pallas_call | solution.py:279
  17.5 0.7 %shard_map.96 = (bf16[8,8,1280]{2,1,0:T(8,128)(2,1)}, bf16[8,32,128]{2,1,0:T(8,128)(2,1)}) custom-call(bf16[8,8,1280]{2,1,0:T(8,128)(2,1)S(1)} %get-tuple-element.6.out, bf16[8,32,128]{2,1,0:T(8,128)(2,1)S(1)} %get-tuple-element.7.fresh), custom_call_target="tpu_custom_call" | custom-call | tf_op jit(solution)/shard_map/pallas_call | solution.py:311

commit v7 on v6

--- a/solution.py
+++ b/solution.py
@@ -111,7 +111,7 @@
 
     pl.semaphore_wait(barrier, n_cols - 1 + n_rows - 1)
     for step in range(1, n_rows):
-        band_copy(by_distance(step)).start()
+        band_copy(by_distance(n_rows - step)).start()
 
     for load in loads[:3]:
         load.wait()
@@ -162,8 +162,11 @@
 
     fresh[...] = fresh_wide[...].reshape(fresh.shape).astype(jnp.bfloat16)
 
+    cells = keyval.shape[1]
+    together = max(size for size in range(1, n_rows + 1) if n_rows % size == 0 and (size == 1 or size * cells <= 1024))
+
     def absorb(state, own, band):
-        block = keyval[band]
+        block = keyval[pl.ds(band * together, together)].reshape(together * cells, keyval.shape[2])
         scores = lax.dot_general(
             block, own, (((1,), (1,)), ((), ())), preferred_element_type=jnp.float32
         )
@@ -185,23 +188,17 @@
         for which in range(count):
             attention[0, first + which] = found[which * strip : (which + 1) * strip]
 
-    if n_rows * chips <= 16:
-        own = queries[...].reshape(n_cols * strip, queries.shape[2])
-        state = absorb(None, own, row)
-        for step in range(1, n_rows):
-            band = by_distance(step)
-            band_arrived(band)
-            state = absorb(state, own, band)
-        keep(state, 0, n_cols)
-    else:
-        for step in range(1, n_rows):
-            band_arrived(by_distance(step))
-
-        @pl.loop(0, chips)
-        def each_pair(index):
-            own = queries[index]
-            state = lax.fori_loop(1, n_rows, lambda band, state: absorb(state, own, band), absorb(None, own, 0))
-            keep(state, index * cores, cores)
+    def attend(index):
+        own = queries[index]
+        state = absorb(None, own, 0)
+        if together < n_rows:
+            state = lax.fori_loop(
+                1, n_rows // together, lambda block, state: absorb(state, own, block), state
+            )
+        keep(state, index * cores, cores)
+
+    for step in range(1, n_rows):
+        band_arrived(by_distance(step))
 
     def att_copy(target, step):
         return pltpu.make_async_remote_copy(
@@ -212,11 +209,13 @@
 
     def serve(step):
         other = lax.rem(chip + step + 1, chips)
+        attend(other)
         for which in range(cores):
             target = other * cores + lax.rem(core + which, cores)
             att_copy(target, (step + 1) * cores + which).start()
 
     repeat(chips - 1, serve)
+    attend(chip)
     if cores > 1:
         att_copy(sibling, 1).start()
     attention[1, col] = attention[0, col]

time: 18.4 us -> 17.3 us (0.940)
  Pallas kernels: 17.6 us -> 16.5 us
    pallas_call x1, Pallas kernels: 16.9 us -> 15.8 us  [shards(): pl.pallas_call(functools.partial(kernel, n_rows, n_cols, cores), out_shap...]
where the time goes in v7:
time: 17.3 us; the launch traced here: 17.1 us
  Pallas kernels  16.5 us (95%)
  between operations  0.64 us (4%)
    pallas_call x1, Pallas kernels, shards(): pl.pallas_call(functools.partial(kernel, n_rows, n_cols, cores), out_shap...  15.8 us
    pallas_call x1, Pallas kernels, shards(): pl.pallas_call(write_back, out_shape=tuple((pltpu.HBM(shape, bf16) for sh...  0.7 us

profile of v7, /device:TPU:0, one launch (start us, length us, event | category | flops | bytes accessed | tf_op | source)
XLA Modules:
  0.0 17.1 jit_solution(10249441460247607930)
XLA Ops:
  0.6 15.8 %shard_map.95 = (bf16[8,8,1280]{2,1,0:T(8,128)(2,1)S(1)}, bf16[8,32,128]{2,1,0:T(8,128)(2,1)S(1)}) custom-call(bf16[8,8,1280]{2,1,0:T(8,128)(2,1)} %hidden_hbm.1, f32[1280]{0:T(1024)} %gain_hbm.1, f32[1280]{0:T(1024)} %bias_hbm.1, bf16[64,1280]{1,0:T(8,128)(2,1)} %bitcast.5, bf16[1280,128]{1,0:T(8,128)(2,1)} %w_keyval_hbm.1, bf16[256,128]{1,0:T(8,128)(2,1)} %bitcast.6, ...), custom_call_target="tpu_custom_call" | custom-call | tf_op jit(solution)/shard_map/pallas_call | solution.py:278
  16.4 0.7 %shard_map.96 = (bf16[8,8,1280]{2,1,0:T(8,128)(2,1)}, bf16[8,32,128]{2,1,0:T(8,128)(2,1)}) custom-call(bf16[8,8,1280]{2,1,0:T(8,128)(2,1)S(1)} %get-tuple-element.6.out, bf16[8,32,128]{2,1,0:T(8,128)(2,1)S(1)} %get-tuple-element.7.fresh), custom_call_target="tpu_custom_call" | custom-call | tf_op jit(solution)/shard_map/pallas_call | solution.py:310

commit v8 on v7

--- a/solution.py
+++ b/solution.py
@@ -129,34 +129,44 @@
         if cores > 1:
             relay_copy(0, part).start()
 
-    def project(index):
-        rows = normed[index]
+    def project(index, part, parts):
+        depth = strip // parts
+        places = [core_index * strip + part * depth for core_index in range(cores)]
+        rows = jnp.concatenate([normed[index, place : place + depth] for place in places], axis=0)
         own = lax.dot_general(
             rows, w_query[...], (((1,), (1,)), ((), ())), preferred_element_type=jnp.float32
         ).astype(jnp.bfloat16)
-        queries[index] = jnp.concatenate([own, jnp.zeros_like(own)], axis=1)
+        own = jnp.concatenate([own, jnp.zeros_like(own)], axis=1)
         both = jnp.dot(rows, w_keyval[...], preferred_element_type=jnp.float32).astype(jnp.bfloat16)
-        keyval[row, pl.ds(pl.multiple_of(index * pair, pair), pair), :] = both
-        wide = both.astype(jnp.float32).reshape(cores, band_rows, strip_cols, both.shape[1])
-        for which in range(cores):
-            fresh_wide[:, index * cores + which] = wide[which]
+        deep = band_rows // parts
+        wide = both.astype(jnp.float32).reshape(cores, deep, strip_cols, both.shape[1])
+        for which, place in enumerate(places):
+            block = slice(which * depth, (which + 1) * depth)
+            queries[index, place : place + depth] = own[block]
+            keyval[row, pl.ds(pl.multiple_of(index * pair + place, depth), depth), :] = both[block]
+            fresh_wide[part * deep : (part + 1) * deep, index * cores + which] = wide[which]
 
     for load in loads[3:5]:
         load.wait()
     if cores > 1:
         for part in range(PIECES):
             relay_copy(0, part).wait_recv()
-    project(chip)
+    project(chip, 0, 1)
 
     def arrive(step):
+        def finish(half):
+            if cores > 1:
+                for part in range(half * PIECES // 2, (half + 1) * PIECES // 2):
+                    relay_copy(step + 1, part).wait_recv()
+            project(lax.rem(chip + chips - step - 1, chips), half, 2)
+
         for part in range(PIECES):
             strip_copy(step, part).wait_recv()
             if cores > 1:
                 relay_copy(step + 1, part).start()
-        if cores > 1:
-            for part in range(PIECES):
-                relay_copy(step + 1, part).wait_recv()
-        project(lax.rem(chip + chips - step - 1, chips))
+            if part == PIECES - 2:
+                finish(0)
+        finish(1)
 
     repeat(chips - 1, arrive)
 
@@ -224,11 +234,19 @@
         load.wait()
     if cores > 1:
         att_copy(sibling, 1).wait_recv()
+
+    def heads_of(index):
+        heads = jnp.concatenate([attention[1, index * cores + which] for which in range(cores)], axis=1)
+        depth = cores * head_size
+        weights = w_out[pl.ds(pl.multiple_of(index * depth, depth), depth), :]
+        return jnp.dot(heads, weights, preferred_element_type=jnp.float32)
+
+    result = hidden[...].astype(jnp.float32).reshape(strip, channels) + out_bias[...].reshape(1, channels)
+    result = result + heads_of(chip)
     for step in range(cores, n_cols):
         att_copy(sibling, step).wait_recv()
-    together_heads = jnp.concatenate([attention[1, head] for head in range(n_cols)], axis=1)
-    result = jnp.dot(together_heads, w_out[...], preferred_element_type=jnp.float32)
-    result = result + out_bias[...].reshape(1, channels) + hidden[...].astype(jnp.float32).reshape(strip, channels)
+    for step in range(1, chips):
+        result = result + heads_of(lax.rem(chip + step, chips))
     out[...] = result.reshape(out.shape).astype(jnp.bfloat16)
 
     for part in range(PIECES):

time: 17.3 us -> 17.4 us (level)
  no operation moved by 1% of the time
where the time goes in v8:
time: 17.4 us; the launch traced here: 17.2 us
  Pallas kernels  16.6 us (95%)
  between operations  0.64 us (4%)
    pallas_call x1, Pallas kernels, shards(): pl.pallas_call(functools.partial(kernel, n_rows, n_cols, cores), out_shap...  15.9 us
    pallas_call x1, Pallas kernels, shards(): pl.pallas_call(write_back, out_shape=tuple((pltpu.HBM(shape, bf16) for sh...  0.7 us

profile of v8, /device:TPU:0, one launch (start us, length us, event | category | flops | bytes accessed | tf_op | source)
XLA Modules:
  0.0 17.2 jit_solution(16826311353642570604)
XLA Ops:
  0.6 15.9 %shard_map.95 = (bf16[8,8,1280]{2,1,0:T(8,128)(2,1)S(1)}, bf16[8,32,128]{2,1,0:T(8,128)(2,1)S(1)}) custom-call(bf16[8,8,1280]{2,1,0:T(8,128)(2,1)} %hidden_hbm.1, f32[1280]{0:T(1024)} %gain_hbm.1, f32[1280]{0:T(1024)} %bias_hbm.1, bf16[64,1280]{1,0:T(8,128)(2,1)} %bitcast.5, bf16[1280,128]{1,0:T(8,128)(2,1)} %w_keyval_hbm.1, bf16[256,128]{1,0:T(8,128)(2,1)} %bitcast.6, ...), custom_call_target="tpu_custom_call" | custom-call | tf_op jit(solution)/shard_map/pallas_call | solution.py:296
  16.5 0.7 %shard_map.96 = (bf16[8,8,1280]{2,1,0:T(8,128)(2,1)}, bf16[8,32,128]{2,1,0:T(8,128)(2,1)}) custom-call(bf16[8,8,1280]{2,1,0:T(8,128)(2,1)S(1)} %get-tuple-element.6.out, bf16[8,32,128]{2,1,0:T(8,128)(2,1)S(1)} %get-tuple-element.7.fresh), custom_call_target="tpu_custom_call" | custom-call | tf_op jit(solution)/shard_map/pallas_call | solution.py:328
